TPU v7x, 32 devices: a whole 2x2x4 slice. The times are simulated.
32 devices in a mesh: src: 8 (over z, core), rcv: 4 (over y, x).
Axes of the slice: x: 2, y: 2, z: 4, core: 2. Of those that a mesh axis runs over, the one named last changes fastest.
Arguments:
- flows: float32 [24, 1024], P(None, 'src'), may hold values from 0.05 to 2
- speeds: float32 [24, 1024], P(None, 'src'), may hold values from 0.3 to 1.2
- seg_length: float32 [8192], P('src'), may hold values from 10 to 100
- relay_list: int32 [8, 8, 16], P('src'), may hold values from -1 to 127, as said below
- seg_slot: int32 [8192], P('src'), may hold values from 0 to 127, as said below
- tile_pairs: int32 [8, 4, 2, 12], P('src', 'rcv'), may hold values from 0 to 7, as said below
- tile_count: int32 [8, 4], P('src', 'rcv'), may hold values from 2 to 12, as said below
- attenuation: bfloat16 [8, 4, 12, 8, 128, 128], P('src', 'rcv')
- dwellings: int32 [4096], P('rcv'), may hold values from 1 to 22
Outputs:
- grad_flows: float32 [24, 1024], P(None, 'src')
- grad_speeds: float32 [24, 1024], P(None, 'src')
- annoyed_count: float32 [], replicated
Inputs may be any that keep to these rules, and one draw needn't show every extreme that they name: relay_list[d, o, :] holds distinct local link indices of owner o first and -1 after them; from 8 to 16 of them are live, and for every d at least one owner has all 16 live. `seg_slot`: each segment's slot names a live entry of its own block's relay list, and every live entry is named by some segment of that block. `tile_pairs`: entry 0 is a segment block below 8, entry 1 a facade block below 8; the pairs of one device are distinct. Only the first tile_count slots of a device are live; some device has all 12 live.
All inputs are finite; a program needn't handle non-finite values.
Results may differ from a plain program's by a relative error of at most 0.0005.
Values may be sent and summed in bfloat16 or wider, within the bound.
No kernel may reach another device: no remote copies, remote signals or barrier semaphores. Data moves between devices by JAX's collectives and lax.ppermute only.
A program may use at most 64 MiB of HBM per device.

v0:
```python
import math

import jax
import jax.numpy as jnp
from jax import lax
from jax.sharding import PartitionSpec as P

rolling_base = [79.7, 85.7, 84.5, 90.2, 97.3, 93.9, 84.1, 74.3]
rolling_slope = [30.0, 41.5, 38.9, 25.7, 32.5, 37.2, 39.0, 40.0]
propel_base = [94.5, 89.2, 88.0, 85.9, 84.2, 86.9, 83.3, 76.1]
propel_slope = [-1.3, 7.2, 7.7, 8.0, 8.0, 8.0, 8.0, 8.0]
aweight_db = [-26.2, -16.1, -8.6, -3.2, 0.0, 1.2, 1.0, -1.1]


def band_column(values):
    return jnp.asarray(values, dtype=jnp.float32)[:, None, None]


def emission(seg_flow, seg_speed, seg_length):
    decibel = math.log(10.0) / 10.0
    speed_kmh = 100.0 * seg_speed
    log_ratio = jnp.log10(speed_kmh / 70.0)
    rolling = jnp.exp(
        decibel * (band_column(rolling_base) - 90.0 + band_column(rolling_slope) * log_ratio[None])
    )
    propel = jnp.exp(
        decibel
        * (
            band_column(propel_base)
            - 90.0
            + band_column(propel_slope) * (speed_kmh[None] - 70.0) / 70.0
        )
    )
    factor = seg_length[None, :] * seg_flow / (100.0 * seg_speed)
    seg_power = factor[None] * (rolling + propel)
    seg_slope = factor[None] * (
        rolling * (band_column(rolling_slope) / 10.0 - 1.0) / seg_speed[None]
        + propel * (math.log(10.0) * band_column(propel_slope) / 7.0 - 1.0 / seg_speed[None])
    )
    return (seg_power, seg_slope)


def band_weight():
    return jnp.exp(math.log(10.0) / 10.0 * band_column(aweight_db))


def dose_response(energy, dwell):
    hour_index = jnp.arange(energy.shape[0], dtype=jnp.int32)
    hour_weight = jnp.where(
        (hour_index >= 7) & (hour_index < 19),
        1.0,
        jnp.where((hour_index >= 19) & (hour_index < 23), math.sqrt(10.0), 10.0),
    ).astype(jnp.float32)
    weighted_sum = jnp.sum(hour_weight[:, None] * (energy + 0.01), axis=0)
    lden_level = 60.0 + 10.0 * jnp.log10(weighted_sum / 24.0)
    people = dwell.astype(jnp.float32)
    annoyed = people * (78.927 - 3.1162 * lden_level + 0.0342 * lden_level * lden_level) / 100.0
    level_slope = people * (-3.1162 + 0.0684 * lden_level) / 100.0 * (10.0 / math.log(10.0))
    level_grad = (level_slope / weighted_sum)[None, :] * hour_weight[:, None]
    return (jnp.sum(annoyed), level_grad)


def shards(
    flows, speeds, seg_length, relay_list, seg_slot, tile_pairs, tile_count, attenuation, dwellings
):
    hour_count = flows.shape[0]
    link_cols = flows.shape[1]
    width = relay_list.shape[2]
    owners = lax.axis_size("src")
    owner_dev = seg_slot // width
    within = seg_slot % width
    table_flow, table_speed = (
        lax.all_gather(flows, "src", axis=1, tiled=True),
        lax.all_gather(speeds, "src", axis=1, tiled=True),
    )
    local_link = relay_list[0][owner_dev, within]
    link_index = owner_dev * link_cols + local_link
    seg_flow = table_flow[:, link_index]
    seg_speed = table_speed[:, link_index]
    seg_power, seg_slope = emission(seg_flow, seg_speed, seg_length)
    weighted = (band_weight() * seg_power).astype(jnp.bfloat16)
    tile_data = attenuation[0, 0]
    tile_list = tile_pairs[0, 0]
    live_tiles = tile_count[0, 0]
    tile_rows = tile_data.shape[-1]
    rcv_cols = dwellings.shape[0]

    def forward_tile(tile_step, energy):
        seg_start = tile_list[0, tile_step] * tile_rows
        rcv_start = tile_list[1, tile_step] * tile_rows
        block = lax.dynamic_slice_in_dim(weighted, seg_start, tile_rows, 2)
        contrib = jnp.einsum(
            "bhs,bsr->hr", block, tile_data[tile_step], preferred_element_type=jnp.float32
        )
        previous = lax.dynamic_slice_in_dim(energy, rcv_start, tile_rows, 1)
        return lax.dynamic_update_slice_in_dim(energy, previous + contrib, rcv_start, 1)

    energy = lax.fori_loop(
        0, live_tiles, forward_tile, jnp.zeros((hour_count, rcv_cols), jnp.float32)
    )
    energy = lax.psum(energy.astype(jnp.bfloat16), "src").astype(jnp.float32)
    annoyed, level_grad = dose_response(energy, dwellings)
    annoyed_count = lax.psum(annoyed, "rcv")
    level_grad = level_grad.astype(jnp.bfloat16)

    def backward_tile(tile_step, seg_back):
        seg_start = tile_list[0, tile_step] * tile_rows
        rcv_start = tile_list[1, tile_step] * tile_rows
        grad_block = lax.dynamic_slice_in_dim(level_grad, rcv_start, tile_rows, 1)
        contrib = jnp.einsum(
            "hr,bsr->bhs", grad_block, tile_data[tile_step], preferred_element_type=jnp.float32
        )
        previous = lax.dynamic_slice_in_dim(seg_back, seg_start, tile_rows, 2)
        return lax.dynamic_update_slice_in_dim(seg_back, previous + contrib, seg_start, 2)

    seg_back = lax.fori_loop(0, live_tiles, backward_tile, jnp.zeros(seg_power.shape, jnp.float32))
    flow_part = jnp.sum(band_weight() * seg_back * seg_power, axis=0) / seg_flow
    speed_part = jnp.sum(band_weight() * seg_back * seg_slope, axis=0)
    flow_part, speed_part = lax.psum((flow_part, speed_part), "rcv")
    full_flow = (
        jnp.zeros((hour_count, owners * link_cols), jnp.float32).at[:, link_index].add(flow_part)
    )
    full_speed = (
        jnp.zeros((hour_count, owners * link_cols), jnp.float32).at[:, link_index].add(speed_part)
    )
    grad_flows, grad_speeds = (
        lax.psum_scatter(full_flow, "src", scatter_dimension=1, tiled=True),
        lax.psum_scatter(full_speed, "src", scatter_dimension=1, tiled=True),
    )
    return (grad_flows, grad_speeds, annoyed_count)


def solution(mesh):
    in_specs = (
        P(None, "src"),
        P(None, "src"),
        P("src"),
        P("src", None, None),
        P("src"),
        P("src", "rcv", None, None),
        P("src", "rcv"),
        P("src", "rcv", None, None, None, None),
        P("rcv"),
    )
    out_specs = (P(None, "src"), P(None, "src"), P())
    return jax.shard_map(shards, mesh=mesh, in_specs=in_specs, out_specs=out_specs, check_vma=False)
```

profile of v0, /device:TPU:0, one launch (start us, length us, event | category | flops | bytes accessed | tf_op | source)
XLA Modules:
  0.0 287.7 jit_solution(4533637767002926467)
XLA Ops:
  7.3 0.7 fusion.24
  8.0 4.8 %gather_fusion = s32[1024]{0:T(1024)S(1)} fusion(s32[8,16]{1,0:T(8,128)S(1)} %bitcast.59, s32[1024]{0:T(1024)S(1)} %fusion.24), kind=kCustom, calls=%fused_computation | custom fusion | bytes 16384 | tf_op jit(solution)/shard_map/gather | solution.py:76
  13.2 16.6 %all_gather.7 = f32[24,1024]{0,1:T(8,128)S(1)} all-gather(f32[24,128]{0,1:T(8,128)S(1)} %copy.55), channel_id=1, replica_groups=mesh['src'=8,'rcv'=4] {'src'}, dimensions={1}, use_global_device_ids=true | all-gather | bytes 110592 | tf_op jit(solution)/shard_map/all_gather | solution.py:74
  29.7 2.8 gather_fusion.2
  32.7 14.7 %all_gather.6 = f32[24,1024]{0,1:T(8,128)S(1)} all-gather(f32[24,128]{0,1:T(8,128)S(1)} %copy.53), channel_id=1, replica_groups=mesh['src'=8,'rcv'=4] {'src'}, dimensions={1}, use_global_device_ids=true | all-gather | bytes 110592 | tf_op jit(solution)/shard_map/all_gather | solution.py:73
  47.5 2.8 gather_fusion.1
  51.1 18.6 %while.20 = (s32[]{:T(128)}, f32[24,1024]{1,0:T(8,128)S(1)}, s32[]{:T(128)}, s32[2,12]{1,0:T(2,128)S(1)}, bf16[8,24,1024]{2,1,0:T(8,128)(2,1)S(1)}, /*index=5*/b...) while((s32[]{:T(128)}, f32[24,1024]{1,0:T(8,128)S(1)}, ...), condition=%wide.region_1.2_spmd, body=%wide.region_0.1_spmd.sunk | while | flops 6294541 | bytes 336147 | solution.py:98
  53.6 1.1 fusion.37
  57.1 1.1 fusion.37
  60.7 1.1 fusion.37
  64.3 1.1 fusion.37
  67.9 1.1 fusion.37
  69.7 38.9 %psum.28 = bf16[24,1024]{1,0:T(8,128)(2,1)S(1)} all-reduce(bf16[24,1024]{1,0:T(8,128)(2,1)S(1)} %convert_element_type.17), channel_id=1, replica_groups=mesh['src'=8,'rcv'=4] {'src'}, use_global_device_ids=true, to_apply=%region_2.3 | all-reduce | flops 24576 | bytes 98304 | tf_op jit(solution)/shard_map/psum | solution.py:101
  108.7 0.6 fusion.21
  109.5 19.1 %while.21 = (s32[]{:T(128)}, f32[8,24,1024]{2,1,0:T(8,128)S(1)}, s32[]{:T(128)}, s32[2,12]{1,0:T(2,128)S(1)}, bf16[12,8,128,128]{3,2,1,0:T(8,128)(2,1)}, /*index...) while((s32[]{:T(128)}, f32[8,24,1024]{2,1,0:T(8,128)S(1)}, ...), condition=%wide.region_5.6_spmd, body=%wide.region_4.5_spmd.sunk | while | flops 6316045 | bytes 465171 | solution.py:116
  112.0 1.2 fusion.40
  115.7 1.2 fusion.40
  119.4 1.2 fusion.40
  123.1 1.2 fusion.40
  126.7 1.2 fusion.40
  128.6 1.4 multiply_reduce_fusion
  130.1 0.7 bitcast_divide_fusion
  130.8 78.4 %all-reduce.3.cloned.1.call-done = (f32[24,1024]{1,0:T(8,128)}, f32[24,1024]{1,0:T(8,128)}) async-done(((f32[24,1024]{1,0:T(8,128)}, f32[24,1024]{1,0:T(8,128)}), (f32[24,1024]{1,0:T(8,128)}, f32[24,1024]{1,0:T(8,128)})) %all-reduce.3.cloned.1.call-update) | async-done | bytes 196624 | tf_op jit(solution)/shard_map/psum | solution.py:119
  209.2 1.1 copy.59
  210.3 6.8 %scatter_custom_fusion.1 = f32[24,1024]{0,1:T(8,128)} fusion(s32[1024]{0:T(1024)S(1)} %get-tuple-element.136, f32[1024,24]{1,0:T(8,128)S(1)} %copy.59, f32[]{:T(128)} %constant.47.clone.1), kind=kCustom, calls=%fused_computation.32 | custom fusion | flops 24576 | bytes 98308 | tf_op jit(solution)/shard_map/scatter-add | solution.py:124
  217.1 1.1 copy.58
  218.2 6.8 %scatter_custom_fusion = f32[24,1024]{0,1:T(8,128)} fusion(s32[1024]{0:T(1024)S(1)} %get-tuple-element.136, f32[1024,24]{1,0:T(8,128)S(1)} %copy.58, f32[]{:T(128)} %constant.47.clone.1), kind=kCustom, calls=%fused_computation.30 | custom fusion | flops 24576 | bytes 98308 | tf_op jit(solution)/shard_map/scatter-add | solution.py:121
  225.1 9.6 %psum.31 = f32[]{:T(128)} all-reduce(f32[]{:T(128)} %get-tuple-element.145), channel_id=1, replica_groups=mesh['src'=8,'rcv'=4] {'rcv'}, use_global_device_ids=true, to_apply=%region_15.16 | all-reduce | flops 1 | bytes 8 | tf_op jit(solution)/shard_map/psum | solution.py:103
  234.6 13.6 %reduce-scatter.5.cloned.1.call-done = f32[24,128]{0,1:T(8,128)} async-done(((f32[24,1024]{0,1:T(8,128)}), f32[24,128]{0,1:T(8,128)}) %reduce-scatter.5.cloned.1.call-update) | async-done | bytes 12304 | tf_op jit(solution)/shard_map/reduce_scatter | solution.py:128
  248.2 1.5 copy.61
  249.7 29.9 %reduce-scatter.3.cloned.1.call-done = f32[24,128]{0,1:T(8,128)} async-done(((f32[24,1024]{0,1:T(8,128)}), f32[24,128]{0,1:T(8,128)}) %reduce-scatter.3.cloned.1.call-update) | async-done | bytes 12304 | tf_op jit(solution)/shard_map/reduce_scatter | solution.py:127
  279.6 1.5 copy.60
  (57 shorter events, 7.4 us)
Async XLA Ops:
  7.2 0.8 copy-start
  7.2 5.6 %copy-start.2 = (s32[1024]{0:T(1024)S(1)}, s32[1024]{0:T(1024)}, u32[]{:S(2)}) copy-start(s32[1024]{0:T(1024)} %param.26) | copy-start | bytes 12292
  7.2 5.8 %copy-start.3 = (f32[24,128]{1,0:T(8,128)S(1)}, f32[24,128]{1,0:T(8,128)}, u32[]{:S(2)}) copy-start(f32[24,128]{1,0:T(8,128)} %param.22) | copy-start | bytes 36868
  7.2 5.9 %copy-start.4 = (f32[24,128]{1,0:T(8,128)S(1)}, f32[24,128]{1,0:T(8,128)}, u32[]{:S(2)}) copy-start(f32[24,128]{1,0:T(8,128)} %param.23) | copy-start | bytes 36868
  7.2 202.0 %all-reduce.3.cloned.1.call-start = ((), (), s32[]{:S(2)}) async-start(), calls=%async_computation.4 | async-start | bytes 393216 | tf_op jit(solution)/shard_map/psum | solution.py:119
  12.8 37.6 %copy-start.5 = (f32[1024]{0:T(1024)S(1)}, f32[1024]{0:T(1024)}, u32[]{:S(2)}) copy-start(f32[1024]{0:T(1024)} %param.24) | copy-start | bytes 12292
  12.8 37.7 %copy-start.7 = (f32[8]{0:T(128)S(1)}, f32[8]{0:T(128)}, u32[]{:S(2)}) copy-start(f32[8]{0:T(128)} %constant.159) | copy-start | bytes 100
  12.9 37.7 %copy-start.8 = (f32[8]{0:T(128)S(1)}, f32[8]{0:T(128)}, u32[]{:S(2)}) copy-start(f32[8]{0:T(128)} %constant.158) | copy-start | bytes 100
  12.9 37.7 %copy-start.9 = (f32[8]{0:T(128)S(1)}, f32[8]{0:T(128)}, u32[]{:S(2)}) copy-start(f32[8]{0:T(128)} %constant.157) | copy-start | bytes 100
  12.9 37.7 %copy-start.10 = (f32[8]{0:T(128)S(1)}, f32[8]{0:T(128)}, u32[]{:S(2)}) copy-start(f32[8]{0:T(128)} %constant.150.clone) | copy-start | bytes 100
  12.9 37.7 %copy-start.11 = (f32[8]{0:T(128)S(1)}, f32[8]{0:T(128)}, u32[]{:S(2)}) copy-start(f32[8]{0:T(128)} %constant.148.clone) | copy-start | bytes 100
  12.9 38.2 %copy-start.1 = (s32[1,1,2,12]{3,2,1,0:T(2,128)S(1)}, s32[1,1,2,12]{3,2,1,0:T(2,128)}, u32[]{:S(2)}) copy-start(s32[1,1,2,12]{3,2,1,0:T(2,128)} %param.27) | copy-start | bytes 292
  32.6 76.2 %copy-start.6 = (s32[1024]{0:T(1024)S(1)}, s32[1024]{0:T(1024)}, u32[]{:S(2)}) copy-start(s32[1024]{0:T(1024)} %param.30) | copy-start | bytes 12292
  51.0 77.6 %copy-start.12 = (f32[8]{0:T(128)S(1)}, f32[8]{0:T(128)}, u32[]{:S(2)}) copy-start(f32[8]{0:T(128)} %constant.162) | copy-start | bytes 100
  51.0 77.6 %copy-start.13 = (f32[8]{0:T(128)S(1)}, f32[8]{0:T(128)}, u32[]{:S(2)}) copy-start(f32[8]{0:T(128)} %constant.161) | copy-start | bytes 100
  130.7 117.4 %reduce-scatter.5.cloned.1.call-start = ((), (), s32[]{:S(2)}) async-start(), calls=%async_computation.3 | async-start | bytes 589824 | tf_op jit(solution)/shard_map/reduce_scatter | solution.py:128
  217.1 62.5 %reduce-scatter.3.cloned.1.call-start = ((), (), s32[]{:S(2)}) async-start(), calls=%async_computation.2 | async-start | bytes 589824 | tf_op jit(solution)/shard_map/reduce_scatter | solution.py:127
Sparse Core Ops, SparseCore 0:
  130.9 78.2 all-reduce.2
  217.2 30.9 reduce-scatter.4
  250.4 29.1 reduce-scatter.2
where the time goes:
time: 290 us; the launch traced here: 288 us
  waiting for transfers between devices  122 us (42%)
  blocking collectives  79.8 us (28%)
  local copies, waits for them, and re-layouts  22.2 us (8%)
  loops' own time  20.4 us (7%)
  other arithmetic  17.7 us (6%)
  between operations  14.1 us (5%)
  matrix products  11.5 us (4%)
    psum x1, waiting for transfers between devices, shards(): flow_part, speed_part = lax.psum((flow_part, speed_part), 'rcv')  78.4 us
    psum x1, blocking collectives, shards(): energy = lax.psum(energy.astype(jnp.bfloat16), 'src').astype(jnp.float32)  38.9 us
    reduce_scatter x1, waiting for transfers between devices, shards(): lax.psum_scatter(full_flow, 'src', scatter_dimension=1, tiled=True)  29.9 us
    all_gather x1, blocking collectives, shards(): lax.all_gather(speeds, 'src', axis=1, tiled=True)  16.6 us
    all_gather x1, blocking collectives, shards(): lax.all_gather(flows, 'src', axis=1, tiled=True)  14.7 us
    scatter-add x2, other arithmetic, shards(): jnp.zeros((hour_count, owners * link_cols), jnp.float32).at[:, link_index]  13.6 us
    reduce_scatter x1, waiting for transfers between devices, shards(): lax.psum_scatter(full_speed, 'src', scatter_dimension=1, tiled=True)  13.6 us
    another operation x1, loops' own time, shards(): lax.fori_loop(0, live_tiles, backward_tile, jnp.zeros(seg_power.shape, jn...  10.2 us
  transfers between devices with their start and end apart: 3, of which 3 were waited for; matrix products, arithmetic and copies ran while one was open for 3% of the time, Pallas kernels for 0%

commit v1 on v0

v1 whole, which is shorter than its diff:
```python
import functools
import math

import jax
import jax.numpy as jnp
from jax import lax
from jax.experimental import pallas as pl
from jax.experimental.pallas import tpu as pltpu
from jax.sharding import PartitionSpec as P

rolling_base = [79.7, 85.7, 84.5, 90.2, 97.3, 93.9, 84.1, 74.3]
rolling_slope = [30.0, 41.5, 38.9, 25.7, 32.5, 37.2, 39.0, 40.0]
propel_base = [94.5, 89.2, 88.0, 85.9, 84.2, 86.9, 83.3, 76.1]
propel_slope = [-1.3, 7.2, 7.7, 8.0, 8.0, 8.0, 8.0, 8.0]
aweight_db = [-26.2, -16.1, -8.6, -3.2, 0.0, 1.2, 1.0, -1.1]

BANDS = 8
LANES = 128
CLASSES = 3
ROOT = math.sqrt(10.0)
DECIBEL = math.log(10.0) / 10.0
NT = (((1,), (1,)), ((), ()))


def iota(shape, axis):
    return lax.broadcasted_iota(jnp.int32, shape, axis)


def hour_class(shape):
    hour = iota(shape, 0)
    day = (hour >= 7) & (hour < 19)
    evening = (hour >= 19) & (hour < 23)
    return jnp.where(day, 0, jnp.where(evening, 1, 2))


def band_terms(band, speed_kmh, log_ratio):
    shift = aweight_db[band] - 90.0
    rolling = jnp.exp(
        DECIBEL * (rolling_base[band] + shift) + (DECIBEL * rolling_slope[band]) * log_ratio
    )
    propel = jnp.exp(
        DECIBEL * (propel_base[band] + shift)
        + (DECIBEL * propel_slope[band] / 70.0) * (speed_kmh - 70.0)
    )
    return rolling, propel


def lane_pick(table, index):
    return jnp.take_along_axis(table, index, axis=1, mode="promise_in_bounds")


def swap_groups(block):
    row, lane = iota((8, LANES), 0), iota((8, LANES), 1)
    block = lane_pick(block, (lane + LANES - 16 * row) % LANES)
    block = jnp.take_along_axis(
        block, (lane // 16 + 8 - row) % 8, axis=0, mode="promise_in_bounds"
    )
    return lane_pick(block, (lane + 16 * row) % LANES)


def split2(value):
    high = value.astype(jnp.bfloat16)
    low = (value - high.astype(jnp.float32)).astype(jnp.bfloat16)
    return high, low


def source_kernel(copies, flow_ref, speed_ref, out_ref):
    flow, speed = flow_ref[...], speed_ref[...]
    kind = hour_class(flow.shape)
    weight = jnp.where(kind == 0, 1.0, jnp.where(kind == 1, ROOT, 10.0))
    speed_kmh = 100.0 * speed
    log_ratio = jnp.log(speed_kmh / 70.0) * (1.0 / math.log(10.0))
    scale = weight * flow / speed_kmh
    row = iota((BANDS, LANES), 0)
    result = jnp.zeros((BANDS, LANES), jnp.float32)
    for band in range(BANDS):
        rolling, propel = band_terms(band, speed_kmh, log_ratio)
        total = jnp.sum(scale * (rolling + propel), axis=0, keepdims=True)
        result = jnp.where(row == band, total, result)
    for copy in range(copies):
        out_ref[copy * BANDS : (copy + 1) * BANDS] = result


def table_kernel(flow_ref, speed_ref, slot_ref, flow_table, speed_table, spread_ref):
    flow, speed = flow_ref[...], speed_ref[...]
    speed_kmh = 100.0 * speed
    log_ratio = jnp.log(speed_kmh / 70.0) * (1.0 / math.log(10.0))
    per_flow = 1.0 / speed_kmh
    factor = flow * per_flow
    inverse = 1.0 / speed
    for band in range(BANDS):
        rolling, propel = band_terms(band, speed_kmh, log_ratio)
        flow_table[band] = per_flow * (rolling + propel)
        speed_table[band] = factor * (
            rolling * (rolling_slope[band] / 10.0 - 1.0) * inverse
            + propel * (math.log(10.0) * propel_slope[band] / 7.0 - inverse)
        )
    blocks = slot_ref.shape[0]
    slots = spread_ref.shape[0]
    for block in range(blocks):
        same = iota((slots, LANES), 0) == slot_ref[block : block + 1]
        spread_ref[:, block * LANES : (block + 1) * LANES] = jnp.where(
            same, 1.0, 0.0
        ).astype(jnp.bfloat16)


def forward_kernel(
    copies, pairs_ref, count_ref, link_ref, relay_ref, slot_ref, length_ref, tile_ref, out_ref,
    seg_scratch, acc_scratch,
):
    owners = link_ref.shape[0] // BANDS
    groups = owners // 8
    lane = iota((BANDS, LANES), 1)
    tables = []
    for group in range(groups):
        index = jnp.broadcast_to(relay_ref[group : group + 1], (BANDS, LANES))
        index = jnp.maximum(index, 0)
        table = jnp.zeros((BANDS, LANES), jnp.float32)
        for member in range(8):
            owner = group * 8 + member
            picked = lane_pick(link_ref[owner * BANDS : (owner + 1) * BANDS], index)
            table = jnp.where(lane // 16 == member, picked, table)
        tables.append(table)
    blocks = slot_ref.shape[0]
    for block in range(blocks):
        slot = jnp.broadcast_to(slot_ref[block : block + 1], (BANDS, LANES))
        value = lane_pick(tables[0], slot % LANES)
        for group in range(1, groups):
            value = jnp.where(slot // LANES == group, lane_pick(tables[group], slot % LANES), value)
        high, low = split2(value * length_ref[block : block + 1])
        seg_scratch[block] = jnp.concatenate([high, low], axis=0)
    acc_scratch[...] = jnp.zeros(acc_scratch.shape, jnp.float32)
    row = iota((2 * BANDS, LANES), 0) % BANDS

    def tile(step, carry):
        seg = seg_scratch[pairs_ref[0, step]]
        facade = pairs_ref[1, step]
        rows = jnp.concatenate(
            [jnp.where(row == band, seg, jnp.zeros_like(seg)) for band in range(BANDS)], axis=1
        )
        tiles = tile_ref[step].reshape(BANDS * LANES, LANES)
        acc_scratch[facade] += jnp.dot(rows, tiles, preferred_element_type=jnp.float32)
        return carry

    lax.fori_loop(0, count_ref[0, 0], tile, 0)
    facades = acc_scratch.shape[0]
    sums = [jnp.sum(acc_scratch[block], axis=0, keepdims=True) for block in range(facades)]
    result = jnp.concatenate(sums, axis=0)
    for copy in range(copies):
        out_ref[copy * facades : (copy + 1) * facades] = result


def backward_kernel(
    hours_weight, receivers, pairs_ref, count_ref, part_ref, people_ref, relay_ref, length_ref,
    spread_ref, tile_ref, out_ref, grad_scratch, acc_scratch,
):
    facades = people_ref.shape[0]
    sources = part_ref.shape[0] // facades
    total = part_ref[0:facades]
    for source in range(1, sources):
        total = total + part_ref[source * facades : (source + 1) * facades]
    total = total + 0.01 * hours_weight
    level = 60.0 + (10.0 / math.log(10.0)) * jnp.log(total / 24.0)
    people = people_ref[...].astype(jnp.float32)
    annoyed = people * (78.927 - 3.1162 * level + 0.0342 * level * level) / 100.0
    annoyed = jnp.sum(annoyed, keepdims=True)
    slope = people * (-3.1162 + 0.0684 * level) / 100.0 * (10.0 / math.log(10.0)) / total
    grads = [slope, slope * ROOT, slope * 10.0]
    pad = jnp.zeros((8, LANES), jnp.float32)
    for block in range(facades):
        rows = [jnp.broadcast_to(g[block : block + 1], (BANDS, LANES)) for g in grads]
        grad_scratch[block] = jnp.concatenate(rows + [pad], axis=0).astype(jnp.bfloat16)
    acc_scratch[...] = jnp.zeros(acc_scratch.shape, jnp.float32)
    row = iota((32, LANES), 0) % BANDS

    def tile(step, carry):
        block = pairs_ref[0, step]
        grad = grad_scratch[pairs_ref[1, step]]
        acc = acc_scratch[block]
        for band in range(BANDS):
            acc = acc + lax.dot_general(
                jnp.where(row == band, grad, jnp.zeros_like(grad)),
                tile_ref[step, band],
                NT,
                preferred_element_type=jnp.float32,
            )
        acc_scratch[block] = acc
        return carry

    lax.fori_loop(0, count_ref[0, 0], tile, 0)
    used = CLASSES * BANDS
    blocks = acc_scratch.shape[0]
    high, low = [], []
    for block in range(blocks):
        value = acc_scratch[block][:used] * length_ref[block : block + 1]
        high_part = value.astype(jnp.bfloat16).astype(jnp.float32)
        high.append(high_part)
        low.append(value - high_part)
    rows = jnp.concatenate(
        [jnp.concatenate(high, axis=1), jnp.concatenate(low, axis=1)], axis=0
    ).astype(jnp.bfloat16)
    slots = lax.dot_general(rows, spread_ref[...], NT, preferred_element_type=jnp.float32)
    slots = slots[:used] + slots[used:]
    owners = out_ref.shape[0] // receivers
    row8, lane8 = iota((8, LANES), 0), iota((8, LANES), 1)
    for group in range(owners // 8):
        lanes = slice(group * LANES, (group + 1) * LANES)
        rows = [
            swap_groups(slots[kind * BANDS : (kind + 1) * BANDS, lanes])
            for kind in range(CLASSES)
        ]
        relay = relay_ref[group * 8 : (group + 1) * 8].astype(jnp.float32)
        for receiver in range(receivers):
            first = receiver * owners + group * 8
            for kind in range(CLASSES):
                out_ref[first : first + 8, kind * LANES : (kind + 1) * LANES] = rows[kind]
            out_ref[first : first + 8, CLASSES * LANES : (CLASSES + 1) * LANES] = relay
            out_ref[first : first + 8, (CLASSES + 1) * LANES :] = jnp.broadcast_to(
                annoyed, (8, LANES)
            )


def finish_kernel(receivers, in_ref, flow_table, speed_table, flow_out, speed_out, count_out):
    owners = in_ref.shape[0] // receivers
    count = in_ref[0:1, (CLASSES + 1) * LANES :]
    for receiver in range(1, receivers):
        first = receiver * owners
        count = count + in_ref[first : first + 1, (CLASSES + 1) * LANES :]
    count_out[...] = count
    row8, lane8 = iota((8, LANES), 0), iota((8, LANES), 1)
    used = CLASSES * BANDS
    links = jnp.zeros((2 * used, LANES), jnp.float32)
    for group in range(owners // 8):
        parts = []
        for kind in range(CLASSES):
            lanes = slice(kind * LANES, (kind + 1) * LANES)
            total = in_ref[group * 8 : group * 8 + 8, lanes]
            for receiver in range(1, receivers):
                first = receiver * owners + group * 8
                total = total + in_ref[first : first + 8, lanes]
            parts.append(swap_groups(total))
        value = jnp.concatenate(parts, axis=0)
        high = value.astype(jnp.bfloat16).astype(jnp.float32)
        rows = jnp.concatenate([high, value - high], axis=0).astype(jnp.bfloat16)
        relay = in_ref[group * 8 : group * 8 + 8, CLASSES * LANES : (CLASSES + 1) * LANES]
        relay = jnp.sum(jnp.where(lane8 // 16 == row8, relay, 0.0), axis=0, keepdims=True)
        relay = relay.astype(jnp.int32)
        spread = jnp.where(iota((LANES, LANES), 0) == relay, 1.0, 0.0).astype(jnp.bfloat16)
        links = links + lax.dot_general(rows, spread, NT, preferred_element_type=jnp.float32)
    links = links[:used] + links[used:]
    kind = hour_class(flow_out.shape)
    flow_sum = jnp.zeros(flow_out.shape, jnp.float32)
    speed_sum = jnp.zeros(flow_out.shape, jnp.float32)
    for band in range(BANDS):
        day, evening, night = [links[k * BANDS + band][None] for k in range(CLASSES)]
        back = jnp.where(kind == 0, day, jnp.where(kind == 1, evening, night))
        flow_sum = flow_sum + back * flow_table[band]
        speed_sum = speed_sum + back * speed_table[band]
    flow_out[...] = flow_sum
    speed_out[...] = speed_sum


def shards(
    flows, speeds, seg_length, relay_list, seg_slot, tile_pairs, tile_count, attenuation, dwellings
):
    sources, receivers = lax.axis_size("src"), lax.axis_size("rcv")
    hours = flows.shape[0]
    width = relay_list.shape[2]
    slots = sources * width
    tile_count_max = attenuation.shape[2]
    f32 = jnp.float32
    blocks, facades = seg_slot.shape[0] // LANES, dwellings.shape[0] // LANES
    hours_weight = sum(
        1.0 if 7 <= h < 19 else (ROOT if 19 <= h < 23 else 10.0) for h in range(hours)
    )
    vmem = pl.BlockSpec(memory_space=pltpu.VMEM)
    smem = pl.BlockSpec(memory_space=pltpu.SMEM)
    tiles = attenuation[0, 0]
    pairs = tile_pairs[0, 0]
    slot_rows = seg_slot.reshape(blocks, LANES)
    length_rows = seg_length.reshape(blocks, LANES)
    people = dwellings.reshape(facades, LANES)
    relay_rows = relay_list[0].reshape(slots // LANES, LANES)
    relay_wide = jnp.tile(relay_list[0], (1, LANES // width))

    power = pl.pallas_call(
        functools.partial(source_kernel, sources),
        out_shape=jax.ShapeDtypeStruct((sources * BANDS, LANES), f32),
        in_specs=[vmem, vmem],
        out_specs=vmem,
        name="source",
    )(flows, speeds)
    power = lax.all_to_all(power, "src", 0, 0, tiled=True)
    flow_table, speed_table, spread = pl.pallas_call(
        table_kernel,
        out_shape=[
            jax.ShapeDtypeStruct((BANDS, hours, LANES), f32),
            jax.ShapeDtypeStruct((BANDS, hours, LANES), f32),
            jax.ShapeDtypeStruct((slots, blocks * LANES), jnp.bfloat16),
        ],
        in_specs=[vmem] * 3,
        out_specs=[vmem] * 3,
        name="tables",
    )(flows, speeds, slot_rows)
    part = pl.pallas_call(
        functools.partial(forward_kernel, sources),
        out_shape=jax.ShapeDtypeStruct((sources * facades, LANES), f32),
        in_specs=[smem, smem] + [vmem] * 5,
        out_specs=vmem,
        scratch_shapes=[
            pltpu.VMEM((blocks, 2 * BANDS, LANES), jnp.bfloat16),
            pltpu.VMEM((facades, 2 * BANDS, LANES), f32),
        ],
        name="forward",
    )(pairs, tile_count, power, relay_rows, slot_rows, length_rows, tiles)
    part = lax.all_to_all(part, "src", 0, 0, tiled=True)
    back = pl.pallas_call(
        functools.partial(backward_kernel, hours_weight, receivers),
        out_shape=jax.ShapeDtypeStruct((receivers * sources, (CLASSES + 2) * LANES), f32),
        in_specs=[smem, smem] + [vmem] * 6,
        out_specs=vmem,
        scratch_shapes=[
            pltpu.VMEM((facades, 32, LANES), jnp.bfloat16),
            pltpu.VMEM((blocks, 32, LANES), f32),
        ],
        name="backward",
    )(pairs, tile_count, part, people, relay_wide, length_rows, spread, tiles)
    back = lax.all_to_all(back, ("rcv", "src"), 0, 0, tiled=True)
    grad_flows, grad_speeds, count = pl.pallas_call(
        functools.partial(finish_kernel, receivers),
        out_shape=[
            jax.ShapeDtypeStruct((hours, LANES), f32),
            jax.ShapeDtypeStruct((hours, LANES), f32),
            jax.ShapeDtypeStruct((1, LANES), f32),
        ],
        in_specs=[vmem] * 3,
        out_specs=[vmem] * 3,
        name="finish",
    )(back, flow_table, speed_table)
    return grad_flows, grad_speeds, count[0, 0]


def solution(mesh):
    in_specs = (
        P(None, "src"),
        P(None, "src"),
        P("src"),
        P("src", None, None),
        P("src"),
        P("src", "rcv", None, None),
        P("src", "rcv"),
        P("src", "rcv", None, None, None, None),
        P("rcv"),
    )
    out_specs = (P(None, "src"), P(None, "src"), P())
    return jax.shard_map(shards, mesh=mesh, in_specs=in_specs, out_specs=out_specs, check_vma=False)
```

time: 290 us -> 47.6 us (0.16)
  waiting for transfers between devices: 122 us -> 7.24 us
  blocking collectives: 79.8 us -> 11.8 us
  loops' own time: 20.4 us -> 0 us
  other arithmetic: 17.7 us -> 0 us
  local copies, waits for them, and re-layouts: 22.2 us -> 4.78 us
  between operations: 14.1 us -> 1.31 us
  Pallas kernels: 0 us -> 12 us
  matrix products: 11.5 us -> 0 us
  starting transfers between devices: 0.12 us -> 9.65 us
    psum x1 -> x0, waiting for transfers between devices: 78.4 us -> none  [shards(): flow_part, speed_part = lax.psum((flow_part, speed_part), 'rcv')]
    psum x2 -> x0, blocking collectives: 48.5 us -> none  [the longest x1 38.9 us: shards(): energy = lax.psum(energy.astype(jnp.bfloat16), 'src').astype(jnp.float32)]
    reduce_scatter x2 -> x0, waiting for transfers between devices: 43.5 us -> none  [the longest x1 29.9 us: shards(): lax.psum_scatter(full_flow, 'src', scatter_dimension=1, tiled=True)]
    all_gather x2 -> x0, blocking collectives: 31.3 us -> none  [the longest x1 16.6 us: shards(): lax.all_gather(speeds, 'src', axis=1, tiled=True)]
    another operation x2 -> x0, loops' own time: 20.4 us -> none  [the longest x1 10.2 us: shards(): lax.fori_loop(0, live_tiles, backward_tile, jnp.zeros(seg_power.shape, jn...]
    scatter-add x2 -> x0, other arithmetic: 13.6 us -> none  [shards(): jnp.zeros((hour_count, owners * link_cols), jnp.float32).at[:, link_index]]
    pallas_call x0 -> x5, Pallas kernels: none -> 12 us  [the longest x1 3.92 us: shards(): pl.pallas_call(functools.partial(backward_kernel, hours_weight, receivers...]
    all_to_all x0 -> x1, blocking collectives: none -> 11.8 us  [shards(): back = lax.all_to_all(back, ('rcv', 'src'), 0, 0, tiled=True)]
  transfers between devices with their start and end apart: 3 -> 2, of which waited for: 3 -> 2; matrix products, arithmetic and copies ran while one was open for 3% -> 4% of each run, Pallas kernels for 0% -> 3%
where the time goes in v1:
time: 47.6 us; the launch traced here: 46.8 us
  Pallas kernels  12 us (25%)
  blocking collectives  11.8 us (25%)
  starting transfers between devices  9.65 us (20%)
  waiting for transfers between devices  7.24 us (15%)
  local copies, waits for them, and re-layouts  4.78 us (10%)
  between operations  1.31 us (3%)
    all_to_all x1, blocking collectives, shards(): back = lax.all_to_all(back, ('rcv', 'src'), 0, 0, tiled=True)  11.8 us
    all_to_all x1, starting transfers between devices, shards(): power = lax.all_to_all(power, 'src', 0, 0, tiled=True)  6.33 us
    pallas_call x1, Pallas kernels, shards(): pl.pallas_call(functools.partial(backward_kernel, hours_weight, receivers...  3.92 us
    all_to_all x1, waiting for transfers between devices, shards(): power = lax.all_to_all(power, 'src', 0, 0, tiled=True)  3.81 us
    all_to_all x1, waiting for transfers between devices, shards(): part = lax.all_to_all(part, 'src', 0, 0, tiled=True)  3.44 us
    all_to_all x1, starting transfers between devices, shards(): part = lax.all_to_all(part, 'src', 0, 0, tiled=True)  3.33 us
    pallas_call x1, Pallas kernels, shards(): pl.pallas_call(functools.partial(forward_kernel, sources), out_shape=jax....  3.24 us
    pallas_call x1, Pallas kernels, shards(): pl.pallas_call(functools.partial(finish_kernel, receivers), out_shape=[ja...  1.88 us
  transfers between devices with their start and end apart: 2, of which 2 were waited for; matrix products, arithmetic and copies ran while one was open for 4% of the time, Pallas kernels for 3%

profile of v1, /device:TPU:0, one launch (start us, length us, event | category | flops | bytes accessed | tf_op | source)
XLA Modules:
  0.0 46.8 jit_solution(6397651681563174297)
XLA Ops:
  0.6 0.0 copy-start.2
  0.6 1.4 %source.1 = f32[64,128]{1,0:T(8,128)} custom-call(f32[24,128]{1,0:T(8,128)} %flow_ref.3, f32[24,128]{1,0:T(8,128)} %speed_ref.3), custom_call_target="tpu_custom_call" | custom-call | tf_op jit(solution)/shard_map/source/pallas_call | solution.py:286
  2.0 6.3 %all-to-all-start = ((f32[8,8,128]{2,1,0:T(8,128)}), f32[8,8,128]{2,1,0:T(8,128)S(1)}, u32[]{:S(2)}, u32[]{:S(2)}) async-start(f32[8,8,128]{2,1,0:T(8,128)} %bitcast.23), calls=%async_computation | async-start | bytes 65536 | tf_op jit(solution)/shard_map/all_to_all | solution.py:293
  9.0 1.3 %reshape_squeeze.3.relay_ref = s32[1,128]{1,0:T(1,128)} reshape(s32[1,8,16]{2,1,0:T(8,128)} %param.12) | data formatting | bytes 1024 | tf_op jit(solution)/shard_map/reshape;squeeze | solution.py:283
  10.3 3.8 %all-to-all-done = f32[8,8,128]{2,1,0:T(8,128)S(1)} async-done(((f32[8,8,128]{2,1,0:T(8,128)}), f32[8,8,128]{2,1,0:T(8,128)S(1)}, u32[]{:S(2)}, u32[]{:S(2)}) %all-to-all-start) | async-done | bytes 32800 | tf_op jit(solution)/shard_map/all_to_all | solution.py:293
  14.1 0.0 copy-start.1
  14.1 0.6 %copy-done.1 = f32[8,8,128]{2,1,0:T(8,128)} copy-done((f32[8,8,128]{2,1,0:T(8,128)}, f32[8,8,128]{2,1,0:T(8,128)S(1)}, u32[]{:S(2)}) %copy-start.1) | copy-done | bytes 32792
  14.7 3.2 %forward.1 = f32[64,128]{1,0:T(8,128)} custom-call(s32[2,12]{1,0:T(2,128)} %bitcast.30, s32[1,1]{1,0:T(1,128)S(6)} %copy.16.count_ref, f32[64,128]{1,0:T(8,128)} %bitcast.22, s32[1,128]{1,0:T(1,128)} %reshape_squeeze.3.relay_ref, s32[8,128]{1,0:T(8,128)} %bitcast.26, f32[8,128]{1,0:T(8,128)} %bitcast.24, bf16[12,8,128,128]{3,2,1,0:T(8,128)(2,1)} %bitcast.16), custom_call_target="tpu_custom_call" | custom-call | tf_op jit(solution)/shard_map/forward/pallas_call | solution.py:305
  17.9 3.3 %all-to-all-start.1 = ((f32[8,8,128]{2,1,0:T(8,128)}), f32[8,8,128]{2,1,0:T(8,128)S(1)}, u32[]{:S(2)}, u32[]{:S(2)}) async-start(f32[8,8,128]{2,1,0:T(8,128)} %bitcast.21), calls=%async_computation.1 | async-start | bytes 65536 | tf_op jit(solution)/shard_map/all_to_all | solution.py:316
  21.3 1.6 %tables.1 = (f32[8,24,128]{2,1,0:T(8,128)}, f32[8,24,128]{2,1,0:T(8,128)}, bf16[128,1024]{1,0:T(8,128)(2,1)}) custom-call(f32[24,128]{1,0:T(8,128)} %flow_ref.3, f32[24,128]{1,0:T(8,128)} %speed_ref.3, s32[8,128]{1,0:T(8,128)} %bitcast.27), custom_call_target="tpu_custom_call" | custom-call | tf_op jit(solution)/shard_map/tables/pallas_call | solution.py:294
  22.8 0.0 copy-done.2
  22.8 0.7 %tile.12.relay_ref = s32[8,128]{1,0:T(8,128)} reshape(s32[8,8,16]{2,1,0:T(8,128)S(1)} %tile.11) | data formatting | bytes 8192 | tf_op jit(solution)/shard_map/tile | solution.py:284
  23.5 3.4 %all-to-all-done.1 = f32[8,8,128]{2,1,0:T(8,128)S(1)} async-done(((f32[8,8,128]{2,1,0:T(8,128)}), f32[8,8,128]{2,1,0:T(8,128)S(1)}, u32[]{:S(2)}, u32[]{:S(2)}) %all-to-all-start.1) | async-done | bytes 32800 | tf_op jit(solution)/shard_map/all_to_all | solution.py:316
  27.0 0.0 copy-start
  27.0 0.6 %copy-done = f32[8,8,128]{2,1,0:T(8,128)} copy-done((f32[8,8,128]{2,1,0:T(8,128)}, f32[8,8,128]{2,1,0:T(8,128)S(1)}, u32[]{:S(2)}) %copy-start) | copy-done | bytes 32792
  27.6 3.9 %backward.1 = f32[32,640]{1,0:T(8,128)} custom-call(s32[2,12]{1,0:T(2,128)} %bitcast.31, s32[1,1]{1,0:T(1,128)S(6)} %copy.16.count_ref, f32[64,128]{1,0:T(8,128)} %bitcast.20, s32[8,128]{1,0:T(8,128)} %bitcast.29, s32[8,128]{1,0:T(8,128)} %tile.12.relay_ref, f32[8,128]{1,0:T(8,128)} %bitcast.25, bf16[128,1024]{1,0:T(8,128)(2,1)} %get-tuple-element.9.spread_ref, ...), custom_call_target="tpu_custom_call" | custom-call | tf_op jit(solution)/shard_map/backward/pallas_call | solution.py:317
  31.5 1.0 %copy.12 = f32[32,1,640]{2,1,0:T(1,128)S(1)} copy(f32[32,1,640]{2,0,1:T(8,128)} %bitcast.18) | data formatting | bytes 163840 | tf_op jit(solution)/shard_map/all_to_all | solution.py:328
  32.5 11.8 %all_to_all.33 = f32[32,1,640]{2,1,0:T(1,128)S(1)} all-to-all(f32[32,1,640]{2,1,0:T(1,128)S(1)} %copy.12), channel_id=1, replica_groups=mesh['src'=8,'rcv'=4] {'rcv','src'}, dimensions={0} | all-to-all | bytes 163840 | tf_op jit(solution)/shard_map/all_to_all | solution.py:328
  44.3 0.6 %copy.15 = f32[32,1,640]{2,0,1:T(8,128)} copy(f32[32,1,640]{2,1,0:T(1,128)S(1)} %all_to_all.33) | data formatting | bytes 163840
  44.9 1.9 %finish.1 = (f32[24,128]{1,0:T(8,128)}, f32[24,128]{1,0:T(8,128)}, f32[1,128]{1,0:T(1,128)}) custom-call(f32[32,640]{1,0:T(8,128)} %bitcast.19, f32[8,24,128]{2,1,0:T(8,128)} %get-tuple-element.10.flow_table, f32[8,24,128]{2,1,0:T(8,128)} %get-tuple-element.11.speed_table), custom_call_target="tpu_custom_call" | custom-call | tf_op jit(solution)/shard_map/finish/pallas_call | solution.py:329
  (1 shorter events, 0.0 us)
Async XLA Ops:
  0.6 22.2 %copy-start.2 = (s32[1,8,16]{2,1,0:T(8,128)S(1)}, s32[1,8,16]{2,1,0:T(8,128)}, u32[]{:S(2)}) copy-start(s32[1,8,16]{2,1,0:T(8,128)} %param.12) | copy-start | bytes 1540
  2.0 12.1 %all-to-all-start = ((f32[8,8,128]{2,1,0:T(8,128)}), f32[8,8,128]{2,1,0:T(8,128)S(1)}, u32[]{:S(2)}, u32[]{:S(2)}) async-start(f32[8,8,128]{2,1,0:T(8,128)} %bitcast.23), calls=%async_computation | async-start | bytes 65536 | tf_op jit(solution)/shard_map/all_to_all | solution.py:293
  14.1 0.6 %copy-start.1 = (f32[8,8,128]{2,1,0:T(8,128)}, f32[8,8,128]{2,1,0:T(8,128)S(1)}, u32[]{:S(2)}) copy-start(f32[8,8,128]{2,1,0:T(8,128)S(1)} %all-to-all-done) | copy-start | bytes 98308
  17.9 9.0 %all-to-all-start.1 = ((f32[8,8,128]{2,1,0:T(8,128)}), f32[8,8,128]{2,1,0:T(8,128)S(1)}, u32[]{:S(2)}, u32[]{:S(2)}) async-start(f32[8,8,128]{2,1,0:T(8,128)} %bitcast.21), calls=%async_computation.1 | async-start | bytes 65536 | tf_op jit(solution)/shard_map/all_to_all | solution.py:316
  27.0 0.6 %copy-start = (f32[8,8,128]{2,1,0:T(8,128)}, f32[8,8,128]{2,1,0:T(8,128)S(1)}, u32[]{:S(2)}) copy-start(f32[8,8,128]{2,1,0:T(8,128)S(1)} %all-to-all-done.1) | copy-start | bytes 98308
